TPU v7x, 32 devices: a whole 2x2x4 slice. The times are simulated.
32 devices in a mesh: depth: 4 (over y, core), cam: 8 (over z, x).
Axes of the slice: x: 2, y: 2, z: 4, core: 2. Of those that a mesh axis runs over, the one named last changes fastest.
Arguments:
- block_rays: int32 [4, 8, 32], P('depth', 'cam'), may hold values from -1 to 127, as said below
- block_offsets: int32 [4, 8, 32], P('depth', 'cam'), may hold values from 0 to 255
- view_order: int32 [8], P('cam'), may hold values from 0 to 1
- ray_frames: float32 [8, 6, 128], P('cam'), may hold values from -6 to 6
- target: float32 [8, 128, 64], P('cam'), may hold values from -3 to 3
- enc_freq: float32 [4, 3, 64], P('depth'), may hold values from -32 to 32
- w_in: bfloat16 [4, 128, 256], P('depth'), may hold values from -0.5 to 0.5
- b_in: float32 [4, 256], P('depth'), may hold values from -3 to 3
- w_mid: bfloat16 [4, 256, 256], P('depth'), may hold values from -0.375 to 0.375
- b_mid: float32 [4, 256], P('depth'), may hold values from -3 to 3
- w_feat: bfloat16 [4, 256, 64], P('depth'), may hold values from -0.375 to 0.375
- w_dens: bfloat16 [4, 256], P('depth'), may hold values from -0.375 to 0.375
Outputs:
- pixels: float32 [8, 128, 64], P('cam', 'depth')
- grad_w_in: float32 [4, 128, 256], P('depth', 'cam')
- grad_b_in: float32 [4, 256], P('depth', 'cam')
- grad_w_mid: float32 [4, 256, 256], P('depth', 'cam')
- grad_b_mid: float32 [4, 256], P('depth', 'cam')
- grad_w_feat: float32 [4, 256, 64], P('depth', 'cam')
- grad_w_dens: float32 [4, 256], P('depth', 'cam')
Inputs may be any that keep to these rules, and one draw needn't show every extreme that they name: `block_rays`: for each region and batch the used slots come first and hold distinct ray numbers of that batch; later slots hold -1. A region's slots over all batches hold at most 64 ray numbers; in every draw some region holds exactly that many, with one batch in it whose 32 slots are all used.
All inputs are finite; a program needn't handle non-finite values.
Results may differ from a plain program's by a relative error of at most 0.011.
Values sent between devices are 32-bit elements; how exact they have to be, the bound alone decides.
A program may use at most 64 MiB of HBM per device.

v0:
```python
import jax
import jax.numpy as jnp
from jax import lax
from jax.sharding import PartitionSpec as P

BLK = 128


step_length = 1.0 / 64.0


def carried_in(part, axis, combine, identity, reverse):
    count = lax.axis_size(axis)
    place = lax.axis_index(axis)
    ahead = count - 1 - place if reverse else place
    gathered = jax.tree.map(lambda a: lax.all_gather(a, axis), part)
    state = jax.tree.map(lambda a, e: jnp.zeros_like(a) + jnp.asarray(e, a.dtype), part, identity)

    def one(step, state):
        source = count - 1 - step if reverse else step
        return combine(
            state, jax.tree.map(lambda a: lax.dynamic_index_in_dim(a, source, 0, False), gathered)
        )

    return lax.fori_loop(0, ahead, one, state)


def contract_rows(left, right):
    return lax.dot_general(
        left, right, (((0,), (0,)), ((), ())), preferred_element_type=jnp.float32
    )


def contract_cols(left, right):
    return lax.dot_general(
        left, right, (((1,), (1,)), ((), ())), preferred_element_type=jnp.float32
    )


def strict_upper(samples):
    rows_index = lax.broadcasted_iota(jnp.int32, (samples, samples), 0)
    cols_index = lax.broadcasted_iota(jnp.int32, (samples, samples), 1)
    return (rows_index < cols_index).astype(jnp.float32)


def block_forward(geometry, offsets, frequency, w_in, b_in, w_mid, b_mid, w_feat, w_dens):
    block_count = offsets.shape[0]
    samples = BLK
    positions = (
        offsets.astype(jnp.float32)[:, None] + jnp.arange(samples, dtype=jnp.float32)[None, :] + 0.5
    ) * step_length
    phases = jnp.zeros((block_count * samples, frequency.shape[1]), jnp.float32)
    for component in range(3):
        coordinate = (
            geometry[component][:, None] + positions * geometry[component + 3][:, None]
        ).reshape(-1)
        phases = phases + coordinate[:, None] * frequency[component][None, :]
    encoded = jnp.concatenate([jnp.sin(phases), jnp.cos(phases)], axis=1).astype(jnp.bfloat16)
    hidden_one = jax.nn.relu(
        jnp.dot(encoded, w_in, preferred_element_type=jnp.float32) + b_in
    ).astype(jnp.bfloat16)
    hidden_two = jax.nn.relu(
        jnp.dot(hidden_one, w_mid, preferred_element_type=jnp.float32) + b_mid
    ).astype(jnp.bfloat16)
    features = jnp.dot(hidden_two, w_feat, preferred_element_type=jnp.float32)
    dens_pre = jnp.dot(hidden_two, w_dens, preferred_element_type=jnp.float32)
    tau_step = (jax.nn.softplus(dens_pre) * step_length).reshape(block_count, samples)
    before = jnp.dot(tau_step, strict_upper(samples), precision=lax.Precision.HIGHEST)
    weights = jnp.exp(-before) * -jnp.expm1(-tau_step)
    feature_grid = features.reshape(block_count, samples, features.shape[1])
    colour = jnp.einsum("bs,bsf->bf", weights, feature_grid, precision=lax.Precision.HIGHEST)
    through = jnp.exp(-(before[:, -1] + tau_step[:, -1]))
    stored = (
        encoded,
        hidden_one,
        hidden_two,
        feature_grid,
        dens_pre,
        tau_step,
        before,
        weights,
        through,
    )
    return (colour, through, stored)


def block_backward(stored, d_colour, d_through, w_mid, w_feat, w_dens):
    encoded, hidden_one, hidden_two, feature_grid, dens_pre, tau_step, before, weights, through = (
        stored
    )
    projected = jnp.einsum("bsf,bf->bs", feature_grid, d_colour, precision=lax.Precision.HIGHEST)
    behind = jnp.dot(projected * weights, strict_upper(BLK).T, precision=lax.Precision.HIGHEST)
    d_tau = projected * jnp.exp(-(before + tau_step)) - behind - (d_through * through)[:, None]
    d_pre = ((d_tau * step_length).reshape(-1) * jax.nn.sigmoid(dens_pre)).astype(jnp.bfloat16)
    d_feat = (
        (weights[:, :, None] * d_colour[:, None, :])
        .reshape(-1, d_colour.shape[1])
        .astype(jnp.bfloat16)
    )
    grad_feat = contract_rows(hidden_two, d_feat)
    grad_dens = jnp.dot(d_pre, hidden_two, preferred_element_type=jnp.float32)
    d_two = (
        contract_cols(d_feat, w_feat)
        + d_pre.astype(jnp.float32)[:, None] * w_dens.astype(jnp.float32)[None, :]
    )
    d_two = jnp.where(hidden_two > 0, d_two, 0.0).astype(jnp.bfloat16)
    grad_mid = contract_rows(hidden_one, d_two)
    grad_bmid = jnp.sum(d_two.astype(jnp.float32), axis=0)
    d_one = jnp.where(hidden_one > 0, contract_cols(d_two, w_mid), 0.0).astype(jnp.bfloat16)
    grad_in = contract_rows(encoded, d_one)
    grad_bin = jnp.sum(d_one.astype(jnp.float32), axis=0)
    return (grad_in, grad_bin, grad_mid, grad_bmid, grad_feat, grad_dens)


def join_pairs(low_pair, high_pair, descending):
    low_colour, low_through = low_pair
    high_colour, high_through = high_pair
    rising = low_colour + low_through[..., None] * high_colour
    falling = high_colour + high_through[..., None] * low_colour
    return (jnp.where(descending, falling, rising), low_through * high_through)


def shards(
    block_rays,
    block_offsets,
    view_order,
    ray_frames,
    target,
    enc_freq,
    w_in,
    b_in,
    w_mid,
    b_mid,
    w_feat,
    w_dens,
):
    slot_rays = block_rays[0, 0]
    slot_offsets = block_offsets[0, 0]
    own_frames = ray_frames[0]
    targets = target[0]
    weights_here = (enc_freq[0], w_in[0], b_in[0], w_mid[0], b_mid[0], w_feat[0], w_dens[0])
    ray_total = own_frames.shape[1]
    feature_count = targets.shape[1]
    occupied = slot_rays >= 0
    ray_index = jnp.maximum(slot_rays, 0)
    descending = view_order[0] == 1
    geometry = jnp.take(own_frames, ray_index, axis=1)
    colour_blk, through_blk, stored = block_forward(geometry, slot_offsets, *weights_here)
    slot_ray = jnp.where(occupied, slot_rays, ray_total)
    own_colour = (
        jnp.zeros((ray_total, feature_count), jnp.float32).at[slot_ray].add(colour_blk, mode="drop")
    )
    own_through = 1.0 - jnp.zeros((ray_total,), jnp.float32).at[slot_ray].add(
        1.0 - through_blk, mode="drop"
    )
    own_pair = (own_colour, own_through)
    pair_zero = (
        jnp.zeros((ray_total, feature_count), jnp.float32),
        jnp.ones((ray_total,), jnp.float32),
    )

    def rising(earlier, later):
        return join_pairs(earlier, later, descending)

    def falling(earlier, later):
        return join_pairs(later, earlier, descending)

    low_pair = carried_in(own_pair, "depth", rising, pair_zero, False)
    high_pair = carried_in(own_pair, "depth", falling, pair_zero, True)
    near_through = jnp.where(descending, high_pair[1], low_pair[1])
    far_colour = jnp.where(descending, low_pair[0], high_pair[0])
    pixels, unused_through = join_pairs(
        join_pairs(low_pair, own_pair, descending), high_pair, descending
    )
    grad_pixel = pixels - targets
    d_colour_ray = near_through[:, None] * grad_pixel
    d_through_ray = near_through * jnp.sum(grad_pixel * far_colour, axis=1)
    d_colour_blk = jnp.take(d_colour_ray, ray_index, axis=0) * occupied[:, None]
    d_through_blk = jnp.take(d_through_ray, ray_index) * occupied
    gradients = block_backward(
        stored, d_colour_blk, d_through_blk, weights_here[3], weights_here[5], weights_here[6]
    )
    reduced = (
        lax.psum_scatter(gradients[0][None], "cam", scatter_dimension=1, tiled=True),
        lax.psum_scatter(gradients[1][None], "cam", scatter_dimension=1, tiled=True),
        lax.psum_scatter(gradients[2][None], "cam", scatter_dimension=1, tiled=True),
        lax.psum_scatter(gradients[3][None], "cam", scatter_dimension=1, tiled=True),
        lax.psum_scatter(gradients[4][None], "cam", scatter_dimension=1, tiled=True),
        lax.psum_scatter(gradients[5][None], "cam", scatter_dimension=1, tiled=True),
    )
    per_device = ray_total // lax.axis_size("depth")
    pixel_out = lax.dynamic_slice_in_dim(
        pixels, lax.axis_index("depth") * per_device, per_device, 0
    )[None]
    return (pixel_out, reduced[0], reduced[1], reduced[2], reduced[3], reduced[4], reduced[5])


def solution(mesh):
    placed = (
        P("depth", "cam", None),
        P("depth", "cam", None),
        P("cam"),
        P("cam", None, None),
        P("cam", None, None),
        P("depth", None, None),
        P("depth", None, None),
        P("depth", None),
        P("depth", None, None),
        P("depth", None),
        P("depth", None, None),
        P("depth", None),
    )
    return jax.shard_map(
        shards,
        mesh=mesh,
        in_specs=placed,
        out_specs=(
            P("cam", "depth", None),
            P("depth", "cam", None),
            P("depth", "cam"),
            P("depth", "cam", None),
            P("depth", "cam"),
            P("depth", "cam", None),
            P("depth", "cam"),
        ),
        check_vma=False,
    )
```

profile of v0, /device:TPU:0, one launch (start us, length us, event | category | flops | bytes accessed | tf_op | source)
XLA Modules:
  0.0 448.3 jit_solution(15541782404567371578)
XLA Ops:
  7.2 0.7 convert_bitcast_fusion
  7.9 1.2 fusion.40
  9.1 0.7 slice_bitcast_fusion.2
  9.8 0.7 copy.41
  10.6 0.5 copy-done.7
  11.1 0.8 copy.43
  11.9 0.6 gather_fusion
  12.6 0.3 slice_reduce_fusion.2
  13.0 4.0 sine_convert_fusion
  17.0 1.7 fusion.7
  18.8 0.7 fusion.10
  19.5 0.6 copy-done.23
  20.1 0.6 fusion.38
  21.6 0.7 copy.45
  22.3 0.6 fusion.49
  23.2 0.8 scatter_custom_fusion.1
  23.9 0.6 broadcast_subtract_fusion
  24.5 6.4 %all-gather.2 = f32[4,1,128]{2,1,0:T(1,128)} all-gather(f32[1,1,128]{2,1,0:T(1,128)S(1)} %get-tuple-element.225), channel_id=3, replica_groups=mesh['depth'=4,'cam'=8] {'depth'}, dimensions={0}, use_global_device_ids=true | all-gather | bytes 2560 | tf_op jit(solution)/shard_map/all_gather | solution.py:16
  31.0 0.7 fusion.21
  31.7 1.7 fusion.54
  33.4 1.3 scatter_custom_fusion
  34.7 6.0 %all-gather = f32[512,64]{1,0:T(8,128)S(1)} all-gather(f32[128,64]{1,0:T(8,128)} %scatter_custom_fusion), channel_id=2, replica_groups=mesh['depth'=4,'cam'=8] {'depth'}, dimensions={0}, use_global_device_ids=true | all-gather | bytes 163840 | tf_op jit(solution)/shard_map/all_gather | solution.py:16
  40.8 0.5 broadcast.204.clone
  41.3 0.6 broadcast.203.clone
  41.9 1.3 fusion.47
  43.2 0.5 broadcast.204.clone.1
  43.7 0.6 broadcast.203.clone.1
  44.3 8.3 %while.26 = (s32[]{:T(128)}, f32[128,64]{1,0:T(8,128)}, f32[128]{0:T(128)}, s32[]{:T(128)}, pred[]{:T(512)}, /*index=5*/f32[4,128,64]{2,1,0:T(8,128)S(1)}, f32[4...) while((s32[]{:T(128)}, f32[128,64]{1,0:T(8,128)}, f32[128]{0:T(128)}, s32[]{:T(128)}, ...), condition=%wide.region_3.4_spmd, body=%wide.region_2.3_spmd.sunk | while | flops 41094 | bytes 102572 | solution.py:25
  44.3 0.7 fusion.77
  45.0 1.6 fusion.78
  46.6 0.5 copy.76
  47.1 0.7 fusion.77
  47.8 1.6 fusion.78
  49.4 0.5 copy.76
  49.9 0.7 fusion.77
  50.6 1.6 fusion.78
  52.1 0.5 copy.76
  52.6 1.2 multiply_reduce_fusion
  53.9 0.7 fusion.52
  54.5 0.8 gather_fusion.2
  55.4 0.9 broadcast_multiply_fusion
  56.3 0.7 gather_fusion.1
  57.0 0.7 select_multiply_fusion
  57.7 1.0 fusion.55
  59.3 1.6 convolution_bitcast_fusion.2
  60.9 0.6 multiply_convert_fusion
  61.6 2.2 convert_reduce_fusion
  63.8 0.8 copy.55
  64.7 4.5 %convert_reduce_fusion.1 = (f32[256]{0:T(256)S(1)}, bf16[4096,256]{1,0:T(8,128)(2,1)}) fusion(bf16[4096,256]{1,0:T(8,128)(2,1)} %get-tuple-element.234, bf16[1,256,256]{2,1,0:T(8,128)(2,1)S(1)} %copy-done, bf16[4096,256]{1,0:T(8,128)(2,1)} %copy-done.23), kind=kOutput, calls=%fused_computation.27 | convolution fusion | flops 542113536 | bytes 6423552 | tf_op jit(solution)/shard_map/dot_general | solution.py:35
  69.2 0.8 copy.53
  70.3 0.6 fusion.11
  70.9 1.4 fusion.56
  72.4 2.8 convolution_bitcast_fusion.1
  75.3 3.0 convolution_bitcast_fusion
  78.4 0.6 dynamic-slice_bitcast_fusion.2
  79.0 44.3 %reduce-scatter.23.cloned.1.call-done = f32[32,1]{1,0:T(8,128)} async-done(((f32[256,1]{1,0:T(8,128)}), f32[32,1]{1,0:T(8,128)}) %reduce-scatter.23.cloned.1.call-update) | async-done | bytes 144
  123.2 1.3 copy.58
  124.5 61.9 %reduce-scatter.21.cloned.1.call-done = f32[32,1]{1,0:T(8,128)} async-done(((f32[256,1]{1,0:T(8,128)}), f32[32,1]{1,0:T(8,128)}) %reduce-scatter.21.cloned.1.call-update) | async-done | bytes 144
  186.5 1.3 copy.56
  187.8 62.0 %reduce-scatter.19.cloned.1.call-done = f32[32,1]{1,0:T(8,128)} async-done(((f32[256,1]{1,0:T(8,128)}), f32[32,1]{1,0:T(8,128)}) %reduce-scatter.19.cloned.1.call-update) | async-done | bytes 144
  249.8 1.3 copy.54
  251.1 62.4 %reduce-scatter.17.cloned.1.call-done = f32[1,32,64]{2,0,1:T(1,128)} async-done(((f32[1,256,64]{2,0,1:T(1,128)}), f32[1,32,64]{2,0,1:T(1,128)}) %reduce-scatter.17.cloned.1.call-update) | async-done | bytes 8208 | tf_op jit(solution)/shard_map/reduce_scatter | solution.py:188
  313.4 63.6 %reduce-scatter.13.cloned.1.call-done = f32[1,16,256]{2,1,0:T(8,128)} async-done(((f32[1,128,256]{2,1,0:T(8,128)}), f32[1,16,256]{2,1,0:T(8,128)}) %reduce-scatter.13.cloned.1.call-update) | async-done | bytes 16400 | tf_op jit(solution)/shard_map/reduce_scatter | solution.py:184
  377.1 64.4 %reduce-scatter.15.cloned.1.call-done = f32[1,32,256]{2,1,0:T(8,128)} async-done(((f32[1,256,256]{2,1,0:T(8,128)}), f32[1,32,256]{2,1,0:T(8,128)}) %reduce-scatter.15.cloned.1.call-update) | async-done | bytes 32784 | tf_op jit(solution)/shard_map/reduce_scatter | solution.py:186
  (74 shorter events, 1.8 us)
Async XLA Ops:
  7.2 11.6 %copy-start = (bf16[1,256,256]{2,1,0:T(8,128)(2,1)S(1)}, bf16[1,256,256]{2,1,0:T(8,128)(2,1)}, u32[]{:S(2)}) copy-start(bf16[1,256,256]{2,1,0:T(8,128)(2,1)} %param.24) | copy-start | bytes 393220
  7.2 116.1 %reduce-scatter.23.cloned.1.call-start = ((), (), s32[]{:S(2)}) async-start(), calls=%async_computation.11 | async-start | bytes 147456
  9.1 3.9 copy-start.20
  10.5 0.6 copy-start.7
  11.1 1.8 copy-start.17
  17.0 1.7 copy-start.1
  17.0 1.7 copy-start.3
  17.0 1.8 copy-start.21
  18.7 1.4 copy-start.23
  18.8 1.3 copy-start.18
  20.1 1.5 copy-start.16
  20.1 10.9 %copy-start.14 = (bf16[1,256,64]{1,2,0:T(8,128)(2,1)S(1)}, bf16[1,256,64]{1,2,0:T(8,128)(2,1)}, u32[]{:S(2)}) copy-start(bf16[1,256,64]{1,2,0:T(8,128)(2,1)} %param.26) | copy-start | bytes 98308
  20.7 10.2 %copy-start.5 = (f32[1,4096]{1,0:T(1,128)}, f32[1,4096]{1,0:T(1,128)S(1)}, u32[]{:S(2)}) copy-start(f32[1,4096]{1,0:T(1,128)S(1)} %fusion.38) | copy-start | bytes 49156
  20.9 10.1 %copy-start.11 = (f32[32,128]{1,0:T(8,128)}, f32[32,128]{1,0:T(8,128)S(1)}, u32[]{:S(2)}) copy-start(f32[32,128]{1,0:T(8,128)S(1)} %fusion.20) | copy-start | bytes 49156
  20.9 10.0 %copy-start.9 = (f32[32,128]{1,0:T(8,128)}, f32[32,128]{1,0:T(8,128)S(1)}, u32[]{:S(2)}) copy-start(f32[32,128]{1,0:T(8,128)S(1)} %fusion.30) | copy-start | bytes 49156
  23.9 9.5 %copy-start.22 = (f32[128]{0:T(128)}, f32[128]{0:T(128)S(1)}, u32[]{:S(2)}) copy-start(f32[128]{0:T(128)S(1)} %scatter_custom_fusion.1) | copy-start | bytes 1540
  52.6 6.2 %copy-start.8 = (s32[32,1]{1,0:T(8,128)S(1)}, s32[32,1]{1,0:T(8,128)}, u32[]{:S(2)}) copy-start(s32[32,1]{1,0:T(8,128)} %copy-done.7) | copy-start | bytes 388
  52.6 6.2 %copy-start.10 = (f32[32,128]{1,0:T(8,128)S(1)}, f32[32,128]{1,0:T(8,128)}, u32[]{:S(2)}) copy-start(f32[32,128]{1,0:T(8,128)} %copy-done.9) | copy-start | bytes 49156
  52.6 6.2 %copy-start.12 = (f32[32,128]{1,0:T(8,128)S(1)}, f32[32,128]{1,0:T(8,128)}, u32[]{:S(2)}) copy-start(f32[32,128]{1,0:T(8,128)} %copy-done.11) | copy-start | bytes 49156
  52.6 6.4 %copy-start.6 = (f32[1,4096]{1,0:T(1,128)S(1)}, f32[1,4096]{1,0:T(1,128)}, u32[]{:S(2)}) copy-start(f32[1,4096]{1,0:T(1,128)} %copy-done.5) | copy-start | bytes 49156
  58.8 2.8 copy-start.19
  58.8 2.8 copy-start.15
  60.9 125.6 %reduce-scatter.21.cloned.1.call-start = ((), (), s32[]{:S(2)}) async-start(), calls=%async_computation.10 | async-start | bytes 147456
  64.7 185.1 %reduce-scatter.19.cloned.1.call-start = ((), (), s32[]{:S(2)}) async-start(), calls=%async_computation.9 | async-start | bytes 147456
  64.7 5.6 %copy-start.13 = (f32[4096]{0:T(1024)S(1)}, f32[4096]{0:T(1024)}, u32[]{:S(2)}) copy-start(f32[4096]{0:T(1024)} %get-tuple-element.217) | copy-start | bytes 49156
  70.0 243.4 %reduce-scatter.17.cloned.1.call-start = ((), (), s32[]{:S(2)}) async-start(), calls=%async_computation.8 | async-start | bytes 147456 | tf_op jit(solution)/shard_map/reduce_scatter | solution.py:188
  70.3 2.1 copy-start.2
  70.3 2.1 copy-start.4
  72.3 3.0 copy-start.24
  72.3 304.7 %reduce-scatter.13.cloned.1.call-start = ((), (), s32[]{:S(2)}) async-start(), calls=%async_computation.6 | async-start | bytes 147456 | tf_op jit(solution)/shard_map/reduce_scatter | solution.py:184
  75.2 366.2 %reduce-scatter.15.cloned.1.call-start = ((), (), s32[]{:S(2)}) async-start(), calls=%async_computation.7 | async-start | bytes 294912 | tf_op jit(solution)/shard_map/reduce_scatter | solution.py:186
Sparse Core Ops, SparseCore 0:
  61.0 62.1 reduce-scatter.22
  126.6 59.8 reduce-scatter.20
  189.8 59.9 reduce-scatter.18
  253.5 59.8 reduce-scatter.16
  317.2 59.8 reduce-scatter.12
  380.8 60.6 reduce-scatter.14
where the time goes:
time: 449 us; the launch traced here: 448 us
  waiting for transfers between devices  359 us (80%)
  other arithmetic  22.9 us (5%)
  matrix products  22.5 us (5%)
  local copies, waits for them, and re-layouts  16.2 us (4%)
  between operations  15.1 us (3%)
  blocking collectives  12.5 us (3%)
    unnamed x9, waiting for transfers between devices  168 us
    reduce_scatter x1, waiting for transfers between devices, shards(): lax.psum_scatter(gradients[2][None], 'cam', scatter_dimension=1, tiled=True)  64.4 us
    reduce_scatter x1, waiting for transfers between devices, shards(): lax.psum_scatter(gradients[0][None], 'cam', scatter_dimension=1, tiled=True)  63.6 us
    reduce_scatter x1, waiting for transfers between devices, shards(): lax.psum_scatter(gradients[4][None], 'cam', scatter_dimension=1, tiled=True)  62.4 us
    all_gather x2, blocking collectives, carried_in(): gathered = jax.tree.map(lambda a: lax.all_gather(a, axis), part)  12.5 us
  transfers between devices with their start and end apart: 6, of which 6 were waited for; matrix products, arithmetic and copies ran while one was open for 5% of the time, Pallas kernels for 0%

commit v1 on v0

v1 whole, which is shorter than its diff:
```python
import functools

import jax
import jax.numpy as jnp
from jax import lax
from jax.experimental import pallas as pl
from jax.experimental.pallas import tpu as pltpu
from jax.sharding import PartitionSpec as P

BLK = 128
STEP = 1.0 / 64.0
MESH = pl.DeviceIdType.MESH
HIGH = lax.Precision.HIGHEST
F32 = jnp.float32
BF16 = jnp.bfloat16

TWO_OVER_PI = 0.6366197723675814
HALF_PI_PARTS = (1.5703125, 4.837512969970703125e-4, 7.549789954891882e-8)


def nn(left, right, precision=None):
    return lax.dot_general(
        left, right, (((1,), (0,)), ((), ())), precision=precision, preferred_element_type=F32
    )


def nt(left, right, precision=None):
    return lax.dot_general(
        left, right, (((1,), (1,)), ((), ())), precision=precision, preferred_element_type=F32
    )


def iota(shape, dim):
    return lax.broadcasted_iota(jnp.int32, shape, dim)


def eye(size, dtype):
    return jnp.where(iota((size, size), 0) == iota((size, size), 1), 1.0, 0.0).astype(dtype)


def sin_cos(angle):
    turns = jnp.floor(angle * TWO_OVER_PI + 0.5)
    quadrant = turns.astype(jnp.int32)
    rest = angle
    for part in HALF_PI_PARTS:
        rest = rest - turns * part
    square = rest * rest
    sine = rest + rest * square * (
        -1.6666654611e-1 + square * (8.3321608736e-3 + square * -1.9515295891e-4)
    )
    cosine = (1.0 - 0.5 * square) + square * square * (
        4.166664568298827e-2 + square * (-1.388731625493765e-3 + square * 2.443315711809948e-5)
    )
    odd = (quadrant & 1) == 1
    sin_out = jnp.where(odd, cosine, sine)
    cos_out = jnp.where(odd, sine, cosine)
    sin_out = jnp.where((quadrant & 2) == 2, -sin_out, sin_out)
    cos_out = jnp.where(((quadrant + 1) & 2) == 2, -cos_out, cos_out)
    return sin_out, cos_out


def join(low, high, falling):
    low_colour, low_through = low
    high_colour, high_through = high
    colour = jnp.where(
        falling, high_colour + high_through * low_colour, low_colour + low_through * high_colour
    )
    return colour, low_through * high_through


def send(src, dst, send_sem, recv_sem, axis, peer):
    copy = pltpu.make_async_remote_copy(
        src_ref=src,
        dst_ref=dst,
        send_sem=send_sem,
        recv_sem=recv_sem,
        device_id={axis: peer},
        device_id_type=MESH,
    )
    copy.start()
    return copy


def kernel(
    regions,
    batches,
    rays_ref,
    offsets_ref,
    view_ref,
    frames_ref,
    target_ref,
    freq_ref,
    w_in_ref,
    b_in_ref,
    w_mid_ref,
    b_mid_ref,
    w_feat_ref,
    w_dens_ref,
    pixels_ref,
    grad_in_ref,
    grad_bin_ref,
    grad_mid_ref,
    grad_bmid_ref,
    grad_feat_ref,
    grad_dens_ref,
    geo,
    aim,
    found,
    enc,
    one,
    two,
    heads,
    pre_in,
    pre_mid,
    pre_feat,
    pre_small,
    got_in,
    got_mid,
    got_feat,
    got_small,
    last_in,
    last_mid,
    last_feat,
    last_small,
    geo_send,
    geo_recv,
    aim_send,
    aim_recv,
    cam_send,
    cam_recv,
    depth_send,
    depth_recv,
    pair_send,
    pair_recv,
    last_send,
    last_recv,
):
    region = lax.axis_index("depth")
    batch = lax.axis_index("cam")
    capacity = rays_ref.shape[2]
    slots = capacity // 4
    ray_total, feat = target_ref.shape[1], target_ref.shape[2]
    half_enc = freq_ref.shape[2]
    hidden = w_mid_ref.shape[1]
    cam_peers = [lax.rem(batch + k, batches) for k in range(1, batches)]
    depth_peers = [lax.rem(region + k, regions) for k in range(1, regions)]

    barrier = pltpu.get_barrier_semaphore()
    for peer in cam_peers:
        pl.semaphore_signal(barrier, inc=1, device_id={"cam": peer}, device_id_type=MESH)
    for peer in depth_peers:
        pl.semaphore_signal(barrier, inc=1, device_id={"depth": peer}, device_id_type=MESH)

    rays_row = rays_ref[0]
    falling_here = view_ref[0] == 1
    named = jnp.maximum(rays_row, 0)
    chosen = jnp.where(iota((ray_total, capacity), 0) == named, 1.0, 0.0)
    geo[batch] = jnp.zeros((8, 128), F32)
    geo[batch, 0:6, 0:capacity] = nn(frames_ref[0], chosen, HIGH)
    geo[batch, 6:7, 0:capacity] = offsets_ref[0].astype(F32)
    geo[batch, 7:8, 0:capacity] = rays_row.astype(F32)
    used = jnp.sum(jnp.where(rays_row >= 0, 1.0, 0.0), axis=1, keepdims=True)
    geo[batch, 6:7, capacity : capacity + 1] = used
    geo[batch, 7:8, capacity : capacity + 1] = jnp.where(
        falling_here, jnp.ones((1, 1), F32), jnp.zeros((1, 1), F32)
    )
    diagonal = iota((capacity, capacity), 0) == iota((capacity, capacity), 1)
    rays_column = jnp.sum(jnp.where(diagonal, named.astype(F32), 0.0), axis=1, keepdims=True)
    chosen_rows = jnp.where(
        iota((capacity, ray_total), 1).astype(F32) == rays_column, 1.0, 0.0
    )
    aim[batch] = nn(chosen_rows, target_ref[0], HIGH)

    pl.semaphore_wait(barrier, batches + regions - 2)
    geo_copies = [
        send(geo.at[batch], geo.at[batch], geo_send.at[k], geo_recv.at[k], "cam", peer)
        for k, peer in enumerate(cam_peers)
    ]
    aim_copies = [
        send(aim.at[batch], aim.at[batch], aim_send.at[k], aim_recv.at[k], "cam", peer)
        for k, peer in enumerate(cam_peers)
    ]

    unit = eye(hidden, BF16)
    w_in_t = nt(unit, w_in_ref[0]).astype(BF16)
    w_mid_t = nt(unit, w_mid_ref[0]).astype(BF16)
    w_feat_t = nt(eye(feat, BF16), w_feat_ref[0]).astype(BF16)
    w_dens_row = w_dens_ref[...]
    heads_t = jnp.concatenate(
        [w_feat_t.astype(F32), jnp.broadcast_to(w_dens_row.astype(F32), (16, hidden))], axis=0
    ).astype(BF16)
    unit_f = eye(hidden, F32)
    b_in_col = jnp.sum(unit_f * b_in_ref[...], axis=1, keepdims=True)
    b_mid_col = jnp.sum(unit_f * b_mid_ref[...], axis=1, keepdims=True)
    w_dens_col = jnp.sum(unit_f * w_dens_row.astype(F32), axis=1, keepdims=True)
    unit_e = eye(half_enc, F32)
    freq_cols = [
        jnp.sum(unit_e * freq_ref[0, c : c + 1, :], axis=1, keepdims=True) for c in range(3)
    ]

    for copy in geo_copies:
        copy.wait()

    wanted = (iota((slots, 1), 0) + slots * batch).astype(F32)
    lane = iota((slots, 128), 1).astype(F32)
    start = jnp.zeros((1, 1), F32)
    picked = jnp.zeros((slots, 8), F32)
    batch_of = jnp.zeros((slots, 1), F32)
    falls = jnp.zeros((slots, 1), F32)
    occupied = jnp.zeros((slots, 1), F32)
    picks = []
    for b in range(batches):
        tile = geo[b]
        count = tile[6:7, capacity : capacity + 1]
        inside = jnp.where((wanted >= start) & (wanted < start + count), 1.0, 0.0)
        pick = jnp.where(lane == wanted - start, 1.0, 0.0) * inside
        picked = picked + nt(pick, tile, HIGH)
        picks.append(pick[:, 0:capacity])
        batch_of = batch_of + inside * float(b)
        falls = falls + inside * tile[7:8, capacity : capacity + 1]
        occupied = occupied + inside
        start = start + count
    number = jnp.where(occupied > 0, picked[:, 7:8], -1.0)

    sample = iota((slots, BLK), 1).astype(F32)
    place = (picked[:, 6:7] + sample + 0.5) * STEP
    coords = [picked[:, c : c + 1] + place * picked[:, c + 3 : c + 4] for c in range(3)]
    for s in range(slots):
        phases = freq_cols[0] * coords[0][s : s + 1]
        for c in (1, 2):
            phases = phases + freq_cols[c] * coords[c][s : s + 1]
        sine, cosine = sin_cos(phases)
        enc[0:half_enc, s * BLK : (s + 1) * BLK] = sine.astype(BF16)
        enc[half_enc : 2 * half_enc, s * BLK : (s + 1) * BLK] = cosine.astype(BF16)
    one[...] = jnp.maximum(nn(w_in_t, enc[...]) + b_in_col, 0.0).astype(BF16)
    two[...] = jnp.maximum(nn(w_mid_t, one[...]) + b_mid_col, 0.0).astype(BF16)
    heads[...] = nn(heads_t, two[...])
    dens = jnp.concatenate(
        [heads[feat : feat + 1, s * BLK : (s + 1) * BLK] for s in range(slots)], axis=0
    )
    tau = (jnp.maximum(dens, 0.0) + jnp.log1p(jnp.exp(-jnp.abs(dens)))) * STEP
    ahead = jnp.where(iota((BLK, BLK), 0) < iota((BLK, BLK), 1), 1.0, 0.0)
    before = nn(tau, ahead, HIGH)
    gone = jnp.exp(-tau)
    weights = jnp.exp(-before) * (jnp.tanh(tau * 0.5) * (1.0 + gone))
    left = jnp.exp(-(before + tau))
    through = left[:, BLK - 1 : BLK]
    row = iota((slots, BLK), 0)
    spread = jnp.concatenate(
        [jnp.where(row == s, weights, 0.0) for s in range(slots)], axis=1
    )
    colour = nt(spread, heads[0:feat, :], HIGH)
    found[region, batch] = jnp.concatenate(
        [
            colour,
            1.0 - through,
            number,
            batch_of,
            jnp.zeros((slots, 128 - feat - 3), F32),
        ],
        axis=1,
    )
    cam_copies = [
        send(
            found.at[region, batch],
            found.at[region, batch],
            cam_send.at[k],
            cam_recv.at[k],
            "cam",
            peer,
        )
        for k, peer in enumerate(cam_peers)
    ]
    for copy in cam_copies:
        copy.wait()
    depth_copies = [
        send(
            found.at[region], found.at[region], depth_send.at[k], depth_recv.at[k], "depth", peer
        )
        for k, peer in enumerate(depth_peers)
    ]
    for copy in aim_copies:
        copy.wait()
    aimed = nn(
        jnp.concatenate(picks, axis=1), aim[...].reshape(batches * capacity, feat), HIGH
    )
    share = pixels_ref.shape[1]
    pixel_keys = (
        iota((share, 1), 0) + (batch * ray_total + region * share)
    ).astype(F32)
    own_keys = jnp.where(occupied > 0, batch_of * float(ray_total) + number, -2.0)
    keys = jnp.concatenate([own_keys, pixel_keys], axis=0)
    rows = slots + share
    falling = (
        jnp.concatenate(
            [falls, jnp.where(falling_here, jnp.ones((share, 1), F32), jnp.zeros((share, 1), F32))],
            axis=0,
        )
        > 0.5
    )
    for copy in depth_copies:
        copy.wait()

    key_lane = iota((16, 128), 1)
    key_maker = jnp.where(
        key_lane == feat + 1, 1.0, jnp.where(key_lane == feat + 2, float(ray_total), 0.0)
    ).astype(BF16)
    pairs = []
    for r in range(regions):
        table = found[r].reshape(batches * slots, 128)
        table_keys = nt(key_maker, table.astype(BF16))[0:1, :]
        match = jnp.where(keys == table_keys, 1.0, 0.0)
        own = nn(match, table, HIGH)
        pairs.append((own[:, 0:feat], 1.0 - own[:, feat : feat + 1]))
    empty = (jnp.zeros((rows, feat), F32), jnp.ones((rows, 1), F32))

    def choose(flag, new, old):
        return tuple(jnp.where(flag, n, o) for n, o in zip(new, old))

    low = high = mine = empty
    for r in range(regions):
        low = choose(r < region, join(low, pairs[r], falling), low)
        mine = choose(r == region, pairs[r], mine)
    for r in reversed(range(regions)):
        high = choose(r > region, join(pairs[r], high, falling), high)
    pixels = join(join(low, mine, falling), high, falling)[0]
    pixels_ref[0] = pixels[slots:, :]

    grad_pixel = pixels[0:slots] - aimed
    near = jnp.where(falling, high[1], low[1])[0:slots] * occupied
    far = jnp.where(falling, low[0], high[0])[0:slots]
    d_colour = near * grad_pixel
    d_through = near * jnp.sum(grad_pixel * far, axis=1, keepdims=True)

    projected_all = nn(d_colour, heads[0:feat, :], HIGH)
    projected = jnp.concatenate(
        [projected_all[s : s + 1, s * BLK : (s + 1) * BLK] for s in range(slots)], axis=0
    )
    after = jnp.where(iota((BLK, BLK), 0) > iota((BLK, BLK), 1), 1.0, 0.0)
    behind = nn(projected * weights, after, HIGH)
    d_tau = projected * left - behind - d_through * through
    d_pre = (d_tau * STEP) * (1.0 / (1.0 + jnp.exp(-dens)))
    d_pre_row = jnp.concatenate([d_pre[s : s + 1] for s in range(slots)], axis=1)
    d_colour_t = nt(eye(feat, F32), d_colour, HIGH)
    d_feat = jnp.concatenate(
        [d_colour_t[:, s : s + 1] * weights[s : s + 1] for s in range(slots)], axis=1
    ).astype(BF16)
    samples = slots * BLK
    d_pre_tile = jnp.where(
        iota((16, samples), 0) == 0, jnp.broadcast_to(d_pre_row, (16, samples)), 0.0
    ).astype(BF16)
    d_heads = jnp.concatenate([d_feat, d_pre_tile], axis=0)

    place_lo = lax.rem(batch, 2)
    place_hi = batch // 2
    other_lo = 1 - place_lo
    partner = place_hi * 2 + other_lo
    chunks = (
        (pre_feat, got_feat, last_feat),
        (pre_mid, got_mid, last_mid),
        (pre_in, got_in, last_in),
        (pre_small, got_small, last_small),
    )

    def send_pair(index):
        part, got, unused = chunks[index]
        return send(
            part.at[other_lo], got, pair_send.at[index], pair_recv.at[index], "cam", partner
        )

    feat_rows = grad_feat_ref.shape[1]
    half_rows = feat_rows // 2
    grad = nt(two[...], d_feat)
    for b in range(batches):
        pre_feat[b % 2, b // 2] = jnp.concatenate(
            [
                grad[b * feat_rows : b * feat_rows + half_rows],
                grad[b * feat_rows + half_rows : (b + 1) * feat_rows],
            ],
            axis=1,
        )
    pair_copies = [send_pair(0)]
    grad_dens = nt(d_pre_tile, two[...])[0:1]

    d_two = nn(
        jnp.concatenate(
            [
                w_feat_ref[0].astype(F32),
                jnp.where(iota((hidden, 16), 1) == 0, w_dens_col, 0.0),
            ],
            axis=1,
        ).astype(BF16),
        d_heads,
    )
    d_two = jnp.where(two[...] > 0, d_two, 0.0).astype(BF16)
    mid_rows = grad_mid_ref.shape[1]
    grad = nt(one[...], d_two)
    for b in range(batches):
        pre_mid[b % 2, b // 2] = grad[b * mid_rows : (b + 1) * mid_rows]
    pair_copies.append(send_pair(1))
    ones = jnp.ones((16, samples), BF16)
    grad_bmid = nt(ones, d_two)[0:1]

    d_one = nn(w_mid_ref[0], d_two)
    d_one = jnp.where(one[...] > 0, d_one, 0.0).astype(BF16)
    in_rows = grad_in_ref.shape[1]
    grad = nt(enc[...], d_one)
    for b in range(batches):
        pre_in[b % 2, b // 2] = grad[b * in_rows : (b + 1) * in_rows]
    pair_copies.append(send_pair(2))
    grad_bin = nt(ones, d_one)[0:1]
    lanes = grad_bin_ref.shape[1]
    for b in range(batches):
        cut = slice(b * lanes, (b + 1) * lanes)
        pre_small[b % 2, b // 2] = jnp.concatenate(
            [
                grad_bin[:, cut],
                grad_bmid[:, cut],
                grad_dens[:, cut],
                jnp.zeros((1, 128 - 3 * lanes), F32),
            ],
            axis=1,
        )
    pair_copies.append(send_pair(3))

    spans = batches // 2
    last_copies = []
    for index, (part, got, last) in enumerate(chunks):
        pair_copies[index].wait()
        got[...] = got[...] + part[place_lo]
        for k in range(1, spans):
            to = lax.rem(place_hi + k, spans)
            last_copies.append(
                send(
                    got.at[to],
                    last.at[k - 1],
                    last_send.at[index, k - 1],
                    last_recv.at[index, k - 1],
                    "cam",
                    to * 2 + place_lo,
                )
            )
    totals = []
    for index, (part, got, last) in enumerate(chunks):
        total = got[place_hi]
        for k in range(1, spans):
            last_copies[index * (spans - 1) + k - 1].wait()
            total = total + last[k - 1]
        totals.append(total)
    grad_feat_ref[0, 0:half_rows] = totals[0][:, 0:feat]
    grad_feat_ref[0, half_rows:feat_rows] = totals[0][:, feat : 2 * feat]
    grad_mid_ref[0] = totals[1]
    grad_in_ref[0] = totals[2]
    grad_bin_ref[...] = totals[3][:, 0:lanes]
    grad_bmid_ref[...] = totals[3][:, lanes : 2 * lanes]
    grad_dens_ref[...] = totals[3][:, 2 * lanes : 3 * lanes]


def shards(regions, batches, *args):
    (rays, offsets, view, frames, target, freq, w_in, b_in, w_mid, b_mid, w_feat, w_dens) = args
    capacity = rays.shape[2]
    slots = capacity // 4
    ray_total, feat = target.shape[1:]
    enc, hidden = w_in.shape[1:]
    samples = slots * BLK
    spans = batches // 2
    in_rows, hid_rows = enc // batches, hidden // batches
    parts = {
        "in": (in_rows, hidden),
        "mid": (hid_rows, hidden),
        "feat": (hid_rows // 2, 2 * feat),
        "small": (1, 128),
    }
    vmem = pl.BlockSpec(memory_space=pltpu.VMEM)
    dma = pltpu.SemaphoreType.DMA
    return pl.pallas_call(
        functools.partial(kernel, regions, batches),
        out_shape=(
            jax.ShapeDtypeStruct((1, ray_total // regions, feat), F32),
            jax.ShapeDtypeStruct((1, in_rows, hidden), F32),
            jax.ShapeDtypeStruct((1, hid_rows), F32),
            jax.ShapeDtypeStruct((1, hid_rows, hidden), F32),
            jax.ShapeDtypeStruct((1, hid_rows), F32),
            jax.ShapeDtypeStruct((1, hid_rows, feat), F32),
            jax.ShapeDtypeStruct((1, hid_rows), F32),
        ),
        in_specs=[vmem, vmem, pl.BlockSpec(memory_space=pltpu.SMEM)] + [vmem] * 9,
        out_specs=(vmem,) * 7,
        scratch_shapes=[
            pltpu.VMEM((batches, 8, 128), F32),
            pltpu.VMEM((batches, capacity, feat), F32),
            pltpu.VMEM((regions, batches, slots, 128), F32),
            pltpu.VMEM((enc, samples), BF16),
            pltpu.VMEM((hidden, samples), BF16),
            pltpu.VMEM((hidden, samples), BF16),
            pltpu.VMEM((feat + 16, samples), F32),
        ]
        + [pltpu.VMEM((2, spans) + shape, F32) for shape in parts.values()]
        + [pltpu.VMEM((spans,) + shape, F32) for shape in parts.values()]
        + [pltpu.VMEM((spans - 1,) + shape, F32) for shape in parts.values()]
        + [dma((batches - 1,))] * 6
        + [dma((regions - 1,))] * 2
        + [dma((4,))] * 2
        + [dma((4, spans - 1))] * 2,
        compiler_params=pltpu.CompilerParams(
            collective_id=0, has_side_effects=True, vmem_limit_bytes=40 * 1024 * 1024
        ),
    )(*args)


def solution(mesh):
    placed = (
        P("depth", "cam", None),
        P("depth", "cam", None),
        P("cam"),
        P("cam", None, None),
        P("cam", None, None),
        P("depth", None, None),
        P("depth", None, None),
        P("depth", None),
        P("depth", None, None),
        P("depth", None),
        P("depth", None, None),
        P("depth", None),
    )
    return jax.shard_map(
        functools.partial(shards, mesh.shape["depth"], mesh.shape["cam"]),
        mesh=mesh,
        in_specs=placed,
        out_specs=(
            P("cam", "depth", None),
            P("depth", "cam", None),
            P("depth", "cam"),
            P("depth", "cam", None),
            P("depth", "cam"),
            P("depth", "cam", None),
            P("depth", "cam"),
        ),
        check_vma=False,
    )
```

time: 449 us -> 42.3 us (0.09)
  waiting for transfers between devices: 359 us -> 0 us
  Pallas kernels: 0 us -> 33.4 us
  other arithmetic: 22.9 us -> 0 us
  matrix products: 22.5 us -> 0 us
  between operations: 15.1 us -> 1.45 us
  blocking collectives: 12.5 us -> 0 us
  local copies, waits for them, and re-layouts: 16.2 us -> 7.13 us
    reduce_scatter x3 -> x0, waiting for transfers between devices: 190 us -> none  [the longest x1 64.4 us: shards(): lax.psum_scatter(gradients[2][None], 'cam', scatter_dimension=1, tiled=True)]
    unnamed x9 -> x0, waiting for transfers between devices: 168 us -> none
    pallas_call x0 -> x1, Pallas kernels: none -> 33.4 us  [shards(): pl.pallas_call(functools.partial(kernel, regions, batches), out_shape=(ja...]
    dot_general x13 -> x0, matrix products: 20.9 us -> none  [the longest x3 7.25 us: contract_rows(): lax.dot_general(left, right, (((0,), (0,)), ((), ())), preferred_element_...]
    all_gather x2 -> x0, blocking collectives: 12.5 us -> none  [carried_in(): gathered = jax.tree.map(lambda a: lax.all_gather(a, axis), part)]
    mul x10 -> x0, other arithmetic: 6.56 us -> none  [the longest x4 3.38 us: join_pairs(): return (jnp.where(descending, falling, rising), low_through * high_through)]
    select_n x4 -> x0, other arithmetic: 4.75 us -> none  [the longest x3 4.68 us: join_pairs(): return (jnp.where(descending, falling, rising), low_through * high_through)]
  transfers between devices with their start and end apart: 6 -> 0, of which waited for: 6 -> 0; matrix products, arithmetic and copies ran while one was open for 5% -> 0% of each run, Pallas kernels for 0% -> 0%
where the time goes in v1:
time: 42.3 us; the launch traced here: 42 us
  Pallas kernels  33.4 us (79%)
  local copies, waits for them, and re-layouts  7.13 us (17%)
  between operations  1.45 us (3%)
    pallas_call x1, Pallas kernels, shards(): pl.pallas_call(functools.partial(kernel, regions, batches), out_shape=(ja...  33.4 us
    unnamed x25, local copies, waits for them, and re-layouts  7.13 us

profile of v1, /device:TPU:0, one launch (start us, length us, event | category | flops | bytes accessed | tf_op | source)
XLA Modules:
  0.0 42.0 jit_solution(2110369221047288281)
XLA Ops:
  0.6 0.0 copy-start
  1.3 0.7 %copy.21.freq_ref = f32[1,3,64]{2,1,0:T(4,128)S(1)} copy(f32[1,3,64]{2,0,1:T(1,128)} %param.17) | data formatting | bytes 1536 | tf_op args[5]
  2.0 0.7 %copy.19.frames_ref = f32[1,6,128]{2,1,0:T(8,128)S(1)} copy(f32[1,6,128]{2,0,1:T(1,128)} %param.15) | data formatting | bytes 6144 | tf_op args[3]
  2.7 0.8 %copy.20.target_ref = f32[1,128,64]{2,1,0:T(8,128)S(1)} copy(f32[1,128,64]{1,2,0:T(8,128)} %param.16) | data formatting | bytes 65536 | tf_op args[4]
  3.5 0.0 copy-start.1
  3.6 0.0 copy-start.2
  3.6 0.0 copy-start.3
  3.6 0.0 copy-start.4
  3.6 0.0 copy-start.5
  3.6 0.0 copy-start.6
  3.6 0.9 %copy.22.w_feat_ref = bf16[1,256,64]{2,1,0:T(8,128)(2,1)S(1)} copy(bf16[1,256,64]{1,2,0:T(8,128)(2,1)} %param.22) | data formatting | bytes 65536 | tf_op args[10]
  4.5 0.0 copy-done
  4.5 0.0 copy-done.1
  4.6 0.0 copy-done.2
  4.6 0.0 copy-done.3
  4.6 0.0 copy-done.4
  4.6 0.0 copy-done.5
  4.6 0.0 copy-done.6
  4.6 33.4 %shard_map.171 = (f32[1,32,64]{2,1,0:T(8,128)S(1)}, f32[1,16,256]{2,1,0:T(8,128)S(1)}, f32[1,32]{1,0:T(1,128)S(1)}, f32[1,32,256]{2,1,0:T(8,128)S(1)}, f32[1,32]...) custom-call(s32[1,1,32]{2,1,0:T(1,128)S(1)} %copy-done.5, s32[1,1,32]{2,1,0:T(1,128)S(1)} %copy-done.6, ...), custom_call_target="tpu_custom_call" | custom-call | tf_op jit(solution)/shard_map/pallas_call | solution.py:476
  38.1 0.6 %copy.31 = f32[1,32,64]{2,1,0:T(8,128)} copy(f32[1,32,64]{2,1,0:T(8,128)S(1)} %get-tuple-element.14) | data formatting | bytes 16384
  38.7 0.6 %copy.32 = f32[1,16,256]{2,1,0:T(8,128)} copy(f32[1,16,256]{2,1,0:T(8,128)S(1)} %get-tuple-element.15) | data formatting | bytes 32768
  39.3 0.5 %copy.33 = f32[1,32]{1,0:T(1,128)} copy(f32[1,32]{1,0:T(1,128)S(1)} %get-tuple-element.16) | data formatting | bytes 256
  39.8 0.6 %copy.34 = f32[1,32,256]{2,1,0:T(8,128)} copy(f32[1,32,256]{2,1,0:T(8,128)S(1)} %get-tuple-element.17) | data formatting | bytes 65536
  40.4 0.5 %copy.35 = f32[1,32]{1,0:T(1,128)} copy(f32[1,32]{1,0:T(1,128)S(1)} %get-tuple-element.18) | data formatting | bytes 256
  40.9 0.6 %copy.36 = f32[1,32,64]{2,1,0:T(8,128)} copy(f32[1,32,64]{2,1,0:T(8,128)S(1)} %get-tuple-element.19) | data formatting | bytes 16384
  41.5 0.5 %copy.37 = f32[1,32]{1,0:T(1,128)} copy(f32[1,32]{1,0:T(1,128)S(1)} %get-tuple-element.20) | data formatting | bytes 256
Async XLA Ops:
  0.6 3.9 %copy-start = (bf16[1,256,256]{2,1,0:T(8,128)(2,1)S(1)}, bf16[1,256,256]{2,1,0:T(8,128)(2,1)}, u32[]{:S(2)}) copy-start(bf16[1,256,256]{2,1,0:T(8,128)(2,1)} %w_mid_ref.1) | copy-start | bytes 393220
  3.5 1.0 %copy-start.1 = (bf16[1,128,256]{2,1,0:T(8,128)(2,1)S(1)}, bf16[1,128,256]{2,1,0:T(8,128)(2,1)}, u32[]{:S(2)}) copy-start(bf16[1,128,256]{2,1,0:T(8,128)(2,1)} %w_in_ref.1) | copy-start | bytes 196612
  3.6 1.0 %copy-start.2 = (f32[1,256]{1,0:T(1,128)S(1)}, f32[1,256]{1,0:T(1,128)}, u32[]{:S(2)}) copy-start(f32[1,256]{1,0:T(1,128)} %b_in_ref.1) | copy-start | bytes 3076
  3.6 1.0 %copy-start.3 = (f32[1,256]{1,0:T(1,128)S(1)}, f32[1,256]{1,0:T(1,128)}, u32[]{:S(2)}) copy-start(f32[1,256]{1,0:T(1,128)} %b_mid_ref.1) | copy-start | bytes 3076
  3.6 1.0 %copy-start.4 = (bf16[1,256]{1,0:T(2,128)(2,1)S(1)}, bf16[1,256]{1,0:T(2,128)(2,1)}, u32[]{:S(2)}) copy-start(bf16[1,256]{1,0:T(2,128)(2,1)} %w_dens_ref.1) | copy-start | bytes 1540
  3.6 1.0 %copy-start.5 = (s32[1,1,32]{2,1,0:T(1,128)S(1)}, s32[1,1,32]{2,1,0:T(1,128)}, u32[]{:S(2)}) copy-start(s32[1,1,32]{2,1,0:T(1,128)} %rays_ref.1) | copy-start | bytes 388
  3.6 1.0 %copy-start.6 = (s32[1,1,32]{2,1,0:T(1,128)S(1)}, s32[1,1,32]{2,1,0:T(1,128)}, u32[]{:S(2)}) copy-start(s32[1,1,32]{2,1,0:T(1,128)} %offsets_ref.1) | copy-start | bytes 388

commit v2 on v1

v2 whole, which is shorter than its diff:
```python
import functools

import jax
import jax.numpy as jnp
from jax import lax
from jax.experimental import pallas as pl
from jax.experimental.pallas import tpu as pltpu
from jax.sharding import PartitionSpec as P

BLK = 128
STEP = 1.0 / 64.0
MESH = pl.DeviceIdType.MESH
HIGH = lax.Precision.HIGHEST
F32 = jnp.float32
BF16 = jnp.bfloat16

TWO_OVER_PI = 0.6366197723675814
HALF_PI_PARTS = (1.5703125, 4.837512969970703125e-4, 7.549789954891882e-8)


def nn(left, right, precision=None):
    return lax.dot_general(
        left, right, (((1,), (0,)), ((), ())), precision=precision, preferred_element_type=F32
    )


def nt(left, right, precision=None):
    return lax.dot_general(
        left, right, (((1,), (1,)), ((), ())), precision=precision, preferred_element_type=F32
    )


def iota(shape, dim):
    return lax.broadcasted_iota(jnp.int32, shape, dim)


def eye(size, dtype):
    return jnp.where(iota((size, size), 0) == iota((size, size), 1), 1.0, 0.0).astype(dtype)


def sin_cos(angle):
    turns = jnp.floor(angle * TWO_OVER_PI + 0.5)
    quadrant = turns.astype(jnp.int32)
    rest = angle
    for part in HALF_PI_PARTS:
        rest = rest - turns * part
    square = rest * rest
    sine = rest + rest * square * (
        -1.6666654611e-1 + square * (8.3321608736e-3 + square * -1.9515295891e-4)
    )
    cosine = (1.0 - 0.5 * square) + square * square * (
        4.166664568298827e-2 + square * (-1.388731625493765e-3 + square * 2.443315711809948e-5)
    )
    odd = (quadrant & 1) == 1
    sin_out = jnp.where(odd, cosine, sine)
    cos_out = jnp.where(odd, sine, cosine)
    sin_out = jnp.where((quadrant & 2) == 2, -sin_out, sin_out)
    cos_out = jnp.where(((quadrant + 1) & 2) == 2, -cos_out, cos_out)
    return sin_out, cos_out


def pieces(value, count):
    found = []
    for _ in range(count):
        piece = value.astype(BF16)
        found.append(piece.astype(F32))
        value = value - found[-1]
    return found


def stack(parts, axis=0):
    return jnp.concatenate(parts, axis=axis).astype(BF16)


def join(low, high, falling):
    low_colour, low_through = low
    high_colour, high_through = high
    colour = jnp.where(
        falling, high_colour + high_through * low_colour, low_colour + low_through * high_colour
    )
    return colour, low_through * high_through


def send(src, dst, send_sem, recv_sem, axis, peer):
    copy = pltpu.make_async_remote_copy(
        src_ref=src,
        dst_ref=dst,
        send_sem=send_sem,
        recv_sem=recv_sem,
        device_id={axis: peer},
        device_id_type=MESH,
    )
    copy.start()
    return copy


def kernel(
    regions,
    batches,
    rays_ref,
    offsets_ref,
    view_ref,
    frames_ref,
    target_ref,
    freq_ref,
    w_in_ref,
    b_in_ref,
    w_mid_ref,
    b_mid_ref,
    w_feat_ref,
    w_dens_ref,
    packed_ref,
    geo,
    aim,
    found,
    enc,
    one,
    two,
    heads,
    got_in,
    got_mid,
    got_feat,
    last_in,
    last_mid,
    last_feat,
    geo_send,
    geo_recv,
    aim_send,
    aim_recv,
    cam_send,
    cam_recv,
    depth_send,
    depth_recv,
    last_send,
    last_recv,
    loads,
):
    region = lax.axis_index("depth")
    batch = lax.axis_index("cam")
    capacity = rays_ref.shape[2]
    spans = batches // 2
    slots = capacity // 2
    place_lo = lax.rem(batch, 2)
    place_hi = batch // 2
    ray_total, feat = target_ref.shape[2], target_ref.shape[1]
    half_enc = freq_ref.shape[2]
    hidden = w_mid_ref.shape[1]
    cam_peers = [lax.rem(batch + k, batches) for k in range(1, batches)]
    depth_peers = [lax.rem(region + k, regions) for k in range(1, regions)]

    in_rows, hid_rows = 2 * half_enc // batches, hidden // batches

    def kept(part, span, rows):
        low_at, high_at = 2 * span * rows, (2 * span + 1) * rows
        return jnp.where(
            place_lo == 0, part[low_at : low_at + rows], part[high_at : high_at + rows]
        )

    def kept_lanes(row, span):
        low_at, high_at = 2 * span * hid_rows, (2 * span + 1) * hid_rows
        return jnp.where(
            place_lo == 0, row[:, low_at : low_at + hid_rows], row[:, high_at : high_at + hid_rows]
        )

    barrier = pltpu.get_barrier_semaphore()
    for peer in cam_peers:
        pl.semaphore_signal(barrier, inc=1, device_id={"cam": peer}, device_id_type=MESH)
    for peer in depth_peers:
        pl.semaphore_signal(barrier, inc=1, device_id={"depth": peer}, device_id_type=MESH)

    for load in loads[0:4]:
        load.wait()
    rays_row = rays_ref[0]
    falling_here = jnp.where(
        jnp.broadcast_to(view_ref[0], (1, 1)) == 1, 1.0, 0.0
    )
    named = jnp.maximum(rays_row, 0)
    chosen = jnp.where(iota((ray_total, capacity), 0) == named, 1.0, 0.0).astype(BF16)
    frames = jnp.concatenate([frames_ref[:, 0, :], jnp.zeros((2, ray_total), F32)], axis=0)
    placed = nn(stack(pieces(frames, 3)), chosen)
    used = jnp.sum(jnp.where(rays_row >= 0, 1.0, 0.0), axis=1, keepdims=True)
    geo[batch] = jnp.zeros((8, 128), F32)
    geo[batch, :, 0:capacity] = placed[0:8] + placed[8:16] + placed[16:24]
    geo[batch, 6:7, 0:capacity] = offsets_ref[0].astype(F32)
    geo[batch, 7:8, 0:capacity] = rays_row.astype(F32)
    geo[batch, 6:7, capacity : capacity + 1] = used
    geo[batch, 7:8, capacity : capacity + 1] = falling_here

    pl.semaphore_wait(barrier, batches + regions - 2)
    geo_copies = [
        send(geo.at[batch], geo.at[batch], geo_send.at[k], geo_recv.at[k], "cam", peer)
        for k, peer in enumerate(cam_peers)
    ]
    loads[4].wait()
    diagonal = iota((capacity, capacity), 0) == iota((capacity, capacity), 1)
    rays_column = jnp.sum(jnp.where(diagonal, named.astype(F32), 0.0), axis=1, keepdims=True)
    chosen_rows = jnp.where(
        iota((capacity, ray_total), 1).astype(F32) == rays_column, 1.0, 0.0
    ).astype(BF16)
    aim[batch] = nt(chosen_rows, stack(pieces(target_ref[0], 2)))
    aim_copies = [
        send(aim.at[batch], aim.at[batch], aim_send.at[k], aim_recv.at[k], "cam", peer)
        for k, peer in enumerate(cam_peers)
    ]

    for load in loads[5:]:
        load.wait()
    samples = slots * BLK
    unit = eye(hidden, BF16)
    unit_feat = eye(feat, BF16)
    w_in_t = nt(unit, w_in_ref[0]).astype(BF16)
    w_mid_t = nt(unit, w_mid_ref[0]).astype(BF16)
    w_dens_row = w_dens_ref[...].astype(F32)
    heads_t = stack(
        [w_feat_ref[0].astype(F32), jnp.broadcast_to(w_dens_row, (16, hidden))]
    )
    rows_f = pieces(b_in_ref[...], 3) + pieces(b_mid_ref[...], 3)
    columns = nt(unit, stack(rows_f + [w_dens_row] + [jnp.zeros((1, hidden), F32)] * 9))
    b_in_col = columns[:, 0:1] + columns[:, 1:2] + columns[:, 2:3]
    b_mid_col = columns[:, 3:4] + columns[:, 4:5] + columns[:, 5:6]
    w_dens_col = columns[:, 6:7]
    freq = jnp.concatenate([freq_ref[:, 0, :], jnp.zeros((5, half_enc), F32)], axis=0)
    freq_t = nt(eye(half_enc, BF16), stack(pieces(freq, 3)))
    freq_cols = [
        freq_t[:, c : c + 1] + freq_t[:, c + 8 : c + 9] + freq_t[:, c + 16 : c + 17]
        for c in range(3)
    ]
    ones = jnp.ones((16, samples), BF16)

    for copy in geo_copies:
        copy.wait()

    wanted = (iota((slots, 1), 0) + slots * place_hi).astype(F32)
    lane = iota((slots, 128), 1).astype(F32)
    start = jnp.zeros((1, 1), F32)
    batch_of = jnp.zeros((slots, 1), F32)
    falls = jnp.zeros((slots, 1), F32)
    occupied = jnp.zeros((slots, 1), F32)
    picks = []
    tiles = []
    for b in range(batches):
        tile = geo[b]
        count = tile[6:7, capacity : capacity + 1]
        inside = jnp.where((wanted >= start) & (wanted < start + count), 1.0, 0.0)
        pick = jnp.where(lane == wanted - start, 1.0, 0.0) * inside
        tiles.append(stack(pieces(tile, 3)))
        picks.append(pick)
        batch_of = batch_of + inside * float(b)
        falls = falls + inside * tile[7:8, capacity : capacity + 1]
        occupied = occupied + inside
        start = start + count
    triple = nt(stack(picks, 1), jnp.concatenate(tiles, axis=1))
    picked = triple[:, 0:8] + triple[:, 8:16] + triple[:, 16:24]
    number = jnp.where(occupied > 0, picked[:, 7:8], -1.0)

    sample = iota((slots, BLK), 1).astype(F32)
    place = (picked[:, 6:7] + sample + 0.5) * STEP
    coords = [picked[:, c : c + 1] + place * picked[:, c + 3 : c + 4] for c in range(3)]
    for s in range(slots):
        phases = freq_cols[0] * coords[0][s : s + 1]
        for c in (1, 2):
            phases = phases + freq_cols[c] * coords[c][s : s + 1]
        sine, cosine = sin_cos(phases)
        enc[0:half_enc, s * BLK : (s + 1) * BLK] = sine.astype(BF16)
        enc[half_enc : 2 * half_enc, s * BLK : (s + 1) * BLK] = cosine.astype(BF16)
    one[...] = jnp.maximum(nn(w_in_t, enc[...]) + b_in_col, 0.0).astype(BF16)
    two[...] = jnp.maximum(nn(w_mid_t, one[...]) + b_mid_col, 0.0).astype(BF16)
    heads[...] = nn(heads_t, two[...])
    dens = jnp.concatenate(
        [heads[feat : feat + 1, s * BLK : (s + 1) * BLK] for s in range(slots)], axis=0
    )
    tau = (jnp.maximum(dens, 0.0) + jnp.log1p(jnp.exp(-jnp.abs(dens)))) * STEP
    ahead = jnp.where(iota((BLK, BLK), 0) < iota((BLK, BLK), 1), 1.0, 0.0)
    before = nn(stack(pieces(tau, 2)), ahead.astype(BF16))
    before = before[0:slots] + before[slots : 2 * slots]
    gone = jnp.exp(-tau)
    weights = jnp.exp(-before) * (jnp.tanh(tau * 0.5) * (1.0 + gone))
    left = jnp.exp(-(before + tau))
    through = left[:, BLK - 1 : BLK]
    weight_parts = jnp.concatenate(pieces(weights, 2), axis=0)
    row_two = iota((2 * slots, BLK), 0) & (slots - 1)
    spread = stack([jnp.where(row_two == s, weight_parts, 0.0) for s in range(slots)], 1)
    crossed = nt(spread, stack(pieces(heads[0:feat, :], 2)))
    colour = (
        crossed[0:slots, 0:feat]
        + crossed[slots : 2 * slots, 0:feat]
        + crossed[0:slots, feat : 2 * feat]
    )
    found[region, place_hi] = jnp.concatenate(
        [
            colour,
            1.0 - through,
            number,
            batch_of,
            jnp.zeros((slots, 128 - feat - 3), F32),
        ],
        axis=1,
    )
    cam_copies = [
        send(
            found.at[region, place_hi],
            found.at[region, place_hi],
            cam_send.at[k],
            cam_recv.at[k],
            "cam",
            lax.rem(place_hi + k + 1, spans) * 2 + place_lo,
        )
        for k in range(spans - 1)
    ]
    seen = nt(two[...], spread)
    seen = seen[:, 0:slots] + seen[:, slots : 2 * slots]
    heads_rows = stack(
        [
            nt(unit, w_feat_ref[0]),
            jnp.where(iota((hidden, 16), 1) == 0, w_dens_col, 0.0),
        ],
        1,
    )
    one_kept = jnp.concatenate(
        [kept(one, h, hid_rows) for h in range(spans)] + [ones], axis=0
    )
    enc_kept = jnp.concatenate([kept(enc, h, in_rows) for h in range(spans)] + [ones], axis=0)
    for h in range(spans):
        got_in[h, in_rows : in_rows + 8] = jnp.zeros((8, hidden), F32)
    slope = 1.0 / (1.0 + jnp.exp(-dens))
    after = jnp.where(iota((BLK, BLK), 0) > iota((BLK, BLK), 1), 1.0, 0.0).astype(BF16)
    for copy in cam_copies:
        copy.wait()
    depth_copies = [
        send(
            found.at[region], found.at[region], depth_send.at[k], depth_recv.at[k], "depth", peer
        )
        for k, peer in enumerate(depth_peers)
    ]
    for copy in aim_copies:
        copy.wait()
    aimed = nn(
        stack([pick[:, 0:capacity] for pick in picks], 1),
        aim[...].reshape(batches * capacity, 2 * feat).astype(BF16),
    )
    aimed = aimed[:, 0:feat] + aimed[:, feat : 2 * feat]
    share = ray_total // regions
    pixel_keys = (
        iota((share, 1), 0) + (batch * ray_total + region * share)
    ).astype(F32)
    own_keys = jnp.where(occupied > 0, batch_of * float(ray_total) + number, -2.0)
    keys = jnp.concatenate([own_keys, pixel_keys], axis=0)
    rows = slots + share
    falling = (
        jnp.concatenate(
            [falls, jnp.broadcast_to(falling_here, (share, 1))],
            axis=0,
        )
        > 0.5
    )
    for copy in depth_copies:
        copy.wait()

    key_lane = iota((16, 128), 1)
    key_maker = jnp.where(
        key_lane == feat + 1, 1.0, jnp.where(key_lane == feat + 2, float(ray_total), 0.0)
    ).astype(BF16)
    pairs = []
    everyone = spans * slots
    tables = found[...].reshape(regions * everyone, 128)
    table_keys = nt(key_maker, tables.astype(BF16))[0:1, :]
    matches = jnp.where(keys == table_keys, 1.0, 0.0).astype(BF16)
    halves = stack(pieces(tables, 2), 1)
    for r in range(regions):
        cut = slice(r * everyone, (r + 1) * everyone)
        own = nn(matches[:, cut], halves[cut])
        own = own[:, 0:128] + own[:, 128:256]
        pairs.append((own[:, 0:feat], 1.0 - own[:, feat : feat + 1]))
    empty = (jnp.zeros((rows, feat), F32), jnp.ones((rows, 1), F32))

    def choose(flag, new, old):
        return tuple(jnp.where(flag, n, o) for n, o in zip(new, old))

    low = high = mine = empty
    for r in range(regions):
        low = choose(r < region, join(low, pairs[r], falling), low)
        mine = choose(r == region, pairs[r], mine)
    for r in reversed(range(regions)):
        high = choose(r > region, join(pairs[r], high, falling), high)
    pixels = join(join(low, mine, falling), high, falling)[0]
    tops = packed_rows(in_rows, hid_rows, share)
    packed_ref[tops[2] : tops[2] + share, 0:feat] = pixels[slots:, :]

    grad_pixel = pixels[0:slots] - aimed
    near = jnp.where(falling, high[1], low[1])[0:slots] * occupied
    far = jnp.where(falling, low[0], high[0])[0:slots]
    d_colour = near * grad_pixel
    d_through = near * jnp.sum(grad_pixel * far, axis=1, keepdims=True)

    d_colour_t = nt(unit_feat, stack(pieces(d_colour, 2)))
    d_colour_t = d_colour_t[:, 0:slots] + d_colour_t[:, slots : 2 * slots]
    projected = []
    d_feat = []
    for s in range(slots):
        column = jnp.broadcast_to(d_colour_t[:, s : s + 1], (feat, BLK))
        projected.append(
            jnp.sum(heads[0:feat, s * BLK : (s + 1) * BLK] * column, axis=0, keepdims=True)
        )
        d_feat.append(column * weights[s : s + 1])
    projected = jnp.concatenate(projected, axis=0)
    behind = nn(stack(pieces(projected * weights, 2)), after)
    behind = behind[0:slots] + behind[slots : 2 * slots]
    d_tau = projected * left - behind - d_through * through
    d_pre = (d_tau * STEP) * slope
    d_pre_row = jnp.concatenate([d_pre[s : s + 1] for s in range(slots)], axis=1)
    d_feat = stack(d_feat, 1)
    d_pre_tile = jnp.where(
        iota((16, samples), 0) == 0, jnp.broadcast_to(d_pre_row, (16, samples)), 0.0
    ).astype(BF16)
    d_heads = jnp.concatenate([d_feat, d_pre_tile], axis=0)
    grad_dens = nt(d_pre_tile, two[...])[0:1]

    chunks = ((got_feat, last_feat), (got_mid, last_mid), (got_in, last_in))
    last_copies = []

    def send_last(index):
        got, last = chunks[index]
        for k in range(1, spans):
            to = lax.rem(place_hi + k, spans)
            last_copies.append(
                send(
                    got.at[to],
                    last.at[k - 1],
                    last_send.at[index, k - 1],
                    last_recv.at[index, k - 1],
                    "cam",
                    to * 2 + place_lo,
                )
            )

    half_rows = hid_rows // 2
    own_rows = jnp.concatenate([kept(seen, h, hid_rows) for h in range(spans)], axis=0)
    grad = nn(own_rows, d_colour, HIGH)
    for h in range(spans):
        top = h * hid_rows
        got_feat[h] = jnp.concatenate(
            [grad[top : top + half_rows], grad[top + half_rows : top + hid_rows]], axis=1
        )
    send_last(0)

    d_two = nn(heads_rows, d_heads)
    d_two = jnp.where(two[...] > 0, d_two, 0.0).astype(BF16)
    grad = nt(one_kept, d_two)
    for h in range(spans):
        got_mid[h] = grad[h * hid_rows : (h + 1) * hid_rows]
    grad_bmid = grad[spans * hid_rows : spans * hid_rows + 1]
    send_last(1)

    d_one = nn(w_mid_ref[0], d_two)
    d_one = jnp.where(one[...] > 0, d_one, 0.0).astype(BF16)
    grad = nt(enc_kept, d_one)
    grad_bin = grad[spans * in_rows : spans * in_rows + 1]
    for h in range(spans):
        got_in[h, 0:in_rows] = grad[h * in_rows : (h + 1) * in_rows]
        for place, row in enumerate((grad_bin, grad_bmid, grad_dens)):
            got_in[h, in_rows + place : in_rows + place + 1, 0:hid_rows] = kept_lanes(row, h)
    send_last(2)

    totals = []
    for index, (got, last) in enumerate(chunks):
        total = got[place_hi]
        for k in range(1, spans):
            last_copies[index * (spans - 1) + k - 1].wait()
            total = total + last[k - 1]
        totals.append(total)
    packed_ref[tops[2] : tops[2] + half_rows, 128 : 128 + feat] = totals[0][:, 0:feat]
    packed_ref[tops[2] + half_rows : tops[2] + hid_rows, 128 : 128 + feat] = totals[0][
        :, feat : 2 * feat
    ]
    packed_ref[tops[1] : tops[1] + hid_rows, :] = totals[1]
    packed_ref[0:in_rows, :] = totals[2][0:in_rows]
    packed_ref[tops[3] : tops[3] + 3, :] = totals[2][in_rows : in_rows + 3]


def round_up(rows):
    return (rows + 7) // 8 * 8


def packed_rows(in_rows, hid_rows, share):
    mid = round_up(in_rows)
    third = mid + round_up(hid_rows)
    small = third + round_up(max(share, hid_rows))
    return (0, mid, third, small, small + 8)


def entry(regions, batches, *refs):
    sources, local, sems = refs[0:12], refs[-13:-1], refs[-1]
    loads = [pltpu.make_async_copy(sources[i], local[i], sems.at[i]) for i in range(12)]
    for load in loads:
        load.start()
    kernel(regions, batches, *local, *refs[12:-13], loads)


def write_out(packed, *refs):
    outs, staged, sems = refs[0:7], refs[7:14], refs[14]
    pixels, w_in, b_in, w_mid, b_mid, w_feat, w_dens = staged
    share, feat = pixels.shape[1:]
    in_rows, hid_rows = w_in.shape[1], w_mid.shape[1]
    tops = packed_rows(in_rows, hid_rows, share)
    w_mid[0] = packed[tops[1] : tops[1] + hid_rows, :]
    w_in[0] = packed[0:in_rows, :]
    pixels[0] = packed[tops[2] : tops[2] + share, 0:feat]
    w_feat[0] = packed[tops[2] : tops[2] + hid_rows, 128 : 128 + feat]
    for place, ref in enumerate((b_in, b_mid, w_dens)):
        ref[...] = packed[tops[3] + place : tops[3] + place + 1, 0:hid_rows]
    copies = [pltpu.make_async_copy(staged[i], outs[i], sems.at[i]) for i in range(7)]
    for copy in copies:
        copy.start()
    for copy in copies:
        copy.wait()


def shards(regions, batches, *args):
    (rays, offsets, view, frames, target, freq, w_in, b_in, w_mid, b_mid, w_feat, w_dens) = args
    frames = jnp.swapaxes(frames, 0, 1)
    freq = jnp.swapaxes(freq, 0, 1)
    target = jnp.swapaxes(target, 1, 2)
    w_feat = jnp.swapaxes(w_feat, 1, 2)
    args = (rays, offsets, view, frames, target, freq, w_in, b_in, w_mid, b_mid, w_feat, w_dens)
    capacity = rays.shape[2]
    slots = capacity // 2
    feat, ray_total = target.shape[1:]
    enc, hidden = w_in.shape[1:]
    samples = slots * BLK
    spans = batches // 2
    in_rows, hid_rows = enc // batches, hidden // batches
    parts = {
        "in": (in_rows + 8, hidden),
        "mid": (hid_rows, hidden),
        "feat": (hid_rows // 2, 2 * feat),
    }
    vmem = pl.BlockSpec(memory_space=pltpu.VMEM)
    dma = pltpu.SemaphoreType.DMA
    out_shape = (
        jax.ShapeDtypeStruct((1, ray_total // regions, feat), F32),
        jax.ShapeDtypeStruct((1, in_rows, hidden), F32),
        jax.ShapeDtypeStruct((1, hid_rows), F32),
        jax.ShapeDtypeStruct((1, hid_rows, hidden), F32),
        jax.ShapeDtypeStruct((1, hid_rows), F32),
        jax.ShapeDtypeStruct((1, hid_rows, feat), F32),
        jax.ShapeDtypeStruct((1, hid_rows), F32),
    )
    height = packed_rows(in_rows, hid_rows, ray_total // regions)[4]
    packed = pl.pallas_call(
        functools.partial(entry, regions, batches),
        out_shape=jax.ShapeDtypeStruct((height, hidden), F32),
        in_specs=[pl.BlockSpec(memory_space=pl.ANY)] * 12,
        out_specs=vmem,
        scratch_shapes=[
            pltpu.VMEM((batches, 8, 128), F32),
            pltpu.VMEM((batches, capacity, 2 * feat), F32),
            pltpu.VMEM((regions, spans, slots, 128), F32),
            pltpu.VMEM((enc, samples), BF16),
            pltpu.VMEM((hidden, samples), BF16),
            pltpu.VMEM((hidden, samples), BF16),
            pltpu.VMEM((feat + 16, samples), F32),
        ]
        + [pltpu.VMEM((spans,) + shape, F32) for shape in parts.values()]
        + [pltpu.VMEM((spans - 1,) + shape, F32) for shape in parts.values()]
        + [dma((batches - 1,))] * 4
        + [dma((spans - 1,))] * 2
        + [dma((regions - 1,))] * 2
        + [dma((3, spans - 1))] * 2
        + [
            (pltpu.SMEM if arg.ndim == 1 else pltpu.VMEM)(arg.shape, arg.dtype) for arg in args
        ]
        + [dma((12,))],
        compiler_params=pltpu.CompilerParams(
            collective_id=0, has_side_effects=True, vmem_limit_bytes=60 * 1024 * 1024
        ),
    )(*args)
    return pl.pallas_call(
        write_out,
        out_shape=out_shape,
        in_specs=[vmem],
        out_specs=(pl.BlockSpec(memory_space=pl.ANY),) * 7,
        scratch_shapes=[pltpu.VMEM(out.shape, out.dtype) for out in out_shape] + [dma((7,))],
    )(packed)


def solution(mesh):
    placed = (
        P("depth", "cam", None),
        P("depth", "cam", None),
        P("cam"),
        P("cam", None, None),
        P("cam", None, None),
        P("depth", None, None),
        P("depth", None, None),
        P("depth", None),
        P("depth", None, None),
        P("depth", None),
        P("depth", None, None),
        P("depth", None),
    )
    return jax.shard_map(
        functools.partial(shards, mesh.shape["depth"], mesh.shape["cam"]),
        mesh=mesh,
        in_specs=placed,
        out_specs=(
            P("cam", "depth", None),
            P("depth", "cam", None),
            P("depth", "cam"),
            P("depth", "cam", None),
            P("depth", "cam"),
            P("depth", "cam", None),
            P("depth", "cam"),
        ),
        check_vma=False,
    )
```

time: 42.3 us -> 33.2 us (0.78)
  local copies, waits for them, and re-layouts: 7.13 us -> 0 us
  Pallas kernels: 33.4 us -> 31.8 us
    unnamed x25 -> x0, local copies, waits for them, and re-layouts: 7.13 us -> none
    pallas_call x1 -> x2, Pallas kernels: 33.4 us -> 31.8 us  [the longest x1 30.2 us: shards(): pl.pallas_call(functools.partial(entry, regions, batches), out_shape=jax....]
where the time goes in v2:
time: 33.2 us; the launch traced here: 33.1 us
  Pallas kernels  31.8 us (96%)
  between operations  1.29 us (4%)
    pallas_call x1, Pallas kernels, shards(): pl.pallas_call(functools.partial(entry, regions, batches), out_shape=jax....  30.2 us
    pallas_call x1, Pallas kernels, shards(): pl.pallas_call(write_out, out_shape=out_shape, in_specs=[vmem], out_specs...  1.59 us

profile of v2, /device:TPU:0, one launch (start us, length us, event | category | flops | bytes accessed | tf_op | source)
XLA Modules:
  0.0 33.1 jit_solution(17692519617954234110)
XLA Ops:
  1.3 30.2 %shard_map.171.packed = f32[88,256]{1,0:T(8,128)} custom-call(s32[1,1,32]{2,1,0:T(1,128)} %refs_0_.1, s32[1,1,32]{2,1,0:T(1,128)} %refs_1_.1, s32[1]{0:T(128)S(6)} %copy.19.refs_2_, f32[6,1,128]{2,1,0:T(1,128)} %bitcast.6, f32[1,64,128]{2,1,0:T(8,128)} %bitcast.4, f32[3,1,64]{2,1,0:T(1,128)} %bitcast.7, bf16[1,128,256]{2,1,0:T(8,128)(2,1)} %refs_6_.1, ...), custom_call_target="tpu_custom_call" | custom-call | tf_op jit(solution)/shard_map/pallas_call | solution.py:549
  31.5 1.6 %shard_map.172 = (f32[1,32,64]{2,1,0:T(8,128)}, f32[1,16,256]{2,1,0:T(8,128)}, f32[1,32]{1,0:T(1,128)}, f32[1,32,256]{2,1,0:T(8,128)}, f32[1,32]{1,0:T(1,128)}, /*index=5*/f32[1,32,64]{2,1,0:T(8,128)}, f32[1,32]{1,0:T(1,128)}) custom-call(f32[88,256]{1,0:T(8,128)} %shard_map.171.packed), custom_call_target="tpu_custom_call" | custom-call | tf_op jit(solution)/shard_map/pallas_call | solution.py:577

commit v3 on v2

--- a/solution.py
+++ b/solution.py
@@ -413,7 +413,6 @@
         iota((16, samples), 0) == 0, jnp.broadcast_to(d_pre_row, (16, samples)), 0.0
     ).astype(BF16)
     d_heads = jnp.concatenate([d_feat, d_pre_tile], axis=0)
-    grad_dens = nt(d_pre_tile, two[...])[0:1]
 
     chunks = ((got_feat, last_feat), (got_mid, last_mid), (got_in, last_in))
     last_copies = []
@@ -450,6 +449,7 @@
         got_mid[h] = grad[h * hid_rows : (h + 1) * hid_rows]
     grad_bmid = grad[spans * hid_rows : spans * hid_rows + 1]
     send_last(1)
+    grad_dens = nt(d_pre_tile, two[...])[0:1]
 
     d_one = nn(w_mid_ref[0], d_two)
     d_one = jnp.where(one[...] > 0, d_one, 0.0).astype(BF16)

time: 33.2 us -> 33 us (level)
  no operation moved by 1% of the time
where the time goes in v3:
time: 33 us; the launch traced here: 32.8 us
  Pallas kernels  31.5 us (95%)
  between operations  1.29 us (4%)
    pallas_call x1, Pallas kernels, shards(): pl.pallas_call(functools.partial(entry, regions, batches), out_shape=jax....  30 us
    pallas_call x1, Pallas kernels, shards(): pl.pallas_call(write_out, out_shape=out_shape, in_specs=[vmem], out_specs...  1.59 us

profile of v3, /device:TPU:0, one launch (start us, length us, event | category | flops | bytes accessed | tf_op | source)
XLA Modules:
  0.0 32.8 jit_solution(840868036560356751)
XLA Ops:
  1.3 30.0 %shard_map.171.packed = f32[88,256]{1,0:T(8,128)} custom-call(s32[1,1,32]{2,1,0:T(1,128)} %refs_0_.1, s32[1,1,32]{2,1,0:T(1,128)} %refs_1_.1, s32[1]{0:T(128)S(6)} %copy.19.refs_2_, f32[6,1,128]{2,1,0:T(1,128)} %bitcast.6, f32[1,64,128]{2,1,0:T(8,128)} %bitcast.4, f32[3,1,64]{2,1,0:T(1,128)} %bitcast.7, bf16[1,128,256]{2,1,0:T(8,128)(2,1)} %refs_6_.1, ...), custom_call_target="tpu_custom_call" | custom-call | tf_op jit(solution)/shard_map/pallas_call | solution.py:549
  31.2 1.6 %shard_map.172 = (f32[1,32,64]{2,1,0:T(8,128)}, f32[1,16,256]{2,1,0:T(8,128)}, f32[1,32]{1,0:T(1,128)}, f32[1,32,256]{2,1,0:T(8,128)}, f32[1,32]{1,0:T(1,128)}, /*index=5*/f32[1,32,64]{2,1,0:T(8,128)}, f32[1,32]{1,0:T(1,128)}) custom-call(f32[88,256]{1,0:T(8,128)} %shard_map.171.packed), custom_call_target="tpu_custom_call" | custom-call | tf_op jit(solution)/shard_map/pallas_call | solution.py:577
